TPU v7x, 32 devices: a whole 2x2x4 slice. The times are simulated.
32 devices in a mesh: groups: 2 (over y), section: 4 (over z), replica: 2 (over x), tensor: 2 (over core).
Axes of the slice: x: 2, y: 2, z: 4, core: 2. Of those that a mesh axis runs over, the one named last changes fastest.
Arguments:
- inflow: bfloat16 [4, 1024, 1152], P('section', ('groups', 'replica')), parts along dimension 1, may hold values from -6 to 6
- fresh_rows: bfloat16 [2, 4, 256, 1152], P(None, ('groups', 'replica'), 'section'), parts along dimension 1, may hold values from -6 to 6
- lin_weight: bfloat16 [4, 1152, 1152], P('section', None, 'tensor'), may hold values from -0.125 to 0.125
- qkv_weight: bfloat16 [4, 3, 1152, 576], P('section', None, None, 'tensor'), may hold values from -2 to 2
- out_weight: bfloat16 [4, 576, 1152], P('section', 'tensor'), may hold values from -0.25 to 0.25
- mod_weight: bfloat16 [4, 128, 2, 1152], P('section', None, None, 'tensor'), may hold values from -0.5 to 0.5
- plan: int32 [3, 4], P(None, 'section'), may hold values from 0 to 5
- timesteps: int32 [6, 4], P(None, ('groups', 'replica')), parts along dimension 1, may hold values from 0 to 999
Outputs:
- settled: float32 [4, 1024, 1152], P('section', ('groups', 'replica'), 'tensor'), parts along dimension 1
There are 2 independent parts, one for each index of `groups`. A program takes and returns all parts, laid end to end along the dimension named above; an argument that names none is the same for every part. Nothing has to cross between parts.
All inputs are finite; a program needn't handle non-finite values.
Results may differ from a plain program's by a relative error of at most 0.039.
Values may be sent and summed in bfloat16 or wider, within the bound.
A program may use at most 64 MiB of HBM per device.

v0:
```python
import math

import jax
import jax.numpy as jnp
from jax import lax
from jax.sharding import PartitionSpec as P

DH = 72
FREQ = 128
TICKS = 3


epsilon = 1e-06


def swapped(value, axis, stride):
    mask = 2**stride
    pairs = [(source, source ^ mask) for source in range(lax.axis_size(axis))]
    return lax.ppermute(value, axis, pairs)


def from_behind(value, axis, steps):
    count = lax.axis_size(axis)
    initial, last = (max(0, -steps), min(count, count - steps))
    return lax.ppermute(value, axis, [(source, source + steps) for source in range(initial, last)])


def timestep_embed(times):
    half_width = FREQ // 2
    frequency = jnp.exp(-math.log(10000.0) * jnp.arange(half_width, dtype=jnp.float32) / half_width)
    phases = times.astype(jnp.float32)[:, None] * frequency[None, :]
    return jnp.concatenate([jnp.cos(phases), jnp.sin(phases)], axis=1)


def mirror(outgoing, section_count):
    routed = outgoing
    for bit_index in range(section_count.bit_length() - 1):
        routed = swapped(routed.astype(jnp.bfloat16), "section", bit_index).astype(routed.dtype)
    return routed


def on_device(inflow, fresh_rows, lin_weight, qkv_weight, out_weight, mod_weight, plan, timesteps):
    section_count = lax.axis_size("section")
    section_index = lax.axis_index("section")
    upper = section_index >= section_count // 2
    arrivals = lax.all_gather(fresh_rows, "section", axis=2, tiled=True)
    current = inflow[0].astype(jnp.float32)
    row_count, width = current.shape
    half_width = lin_weight.shape[2]
    image_count = timesteps.shape[1]
    token_count = row_count // image_count
    head_cols = out_weight.shape[1]
    heads_here = head_cols // DH
    column = lax.axis_index("tensor") * half_width
    arrivals = arrivals.reshape(arrivals.shape[0], row_count, width).astype(jnp.float32)
    micro_ids = lax.broadcasted_iota(jnp.int32, timesteps.shape, 0)
    output_half = lax.dynamic_slice_in_dim(current, column, half_width, 1)
    for tick_index in range(TICKS):
        product = jnp.dot(
            current.astype(jnp.bfloat16), lin_weight[0], preferred_element_type=jnp.float32
        )
        incoming = mirror(product, section_count)
        own_cols = lax.dynamic_slice_in_dim(current, column, half_width, 1)
        hidden_half = jnp.where(upper, product + incoming, own_cols)
        chosen = plan[tick_index, 0]
        times = jnp.sum(jnp.where(micro_ids == chosen, timesteps, 0), axis=0)
        mod_half = (
            jnp.einsum(
                "if,fcd->icd",
                timestep_embed(times),
                mod_weight[0].astype(jnp.float32),
                precision=lax.Precision.HIGHEST,
            )
            .astype(jnp.bfloat16)
            .astype(jnp.float32)
        )
        hidden, modulation = (
            lax.all_gather(hidden_half.astype(jnp.bfloat16), "tensor", axis=1, tiled=True).astype(
                hidden_half.dtype
            ),
            lax.all_gather(mod_half.astype(jnp.bfloat16), "tensor", axis=2, tiled=True).astype(
                mod_half.dtype
            ),
        )
        values_f = hidden.reshape(image_count, token_count, width)
        centred = values_f - jnp.mean(values_f, axis=-1, keepdims=True)
        variance = jnp.mean(centred * centred, axis=-1, keepdims=True)
        normed = centred * lax.rsqrt(variance + epsilon)
        scaling = modulation[:, 0][:, None, :]
        mixed = (normed * (1.0 + scaling)).astype(jnp.bfloat16).reshape(row_count, width)
        projected = [
            jnp.dot(mixed, qkv_weight[0, index], preferred_element_type=jnp.float32)
            .astype(jnp.bfloat16)
            .reshape(image_count, token_count, heads_here, DH)
            for index in range(3)
        ]
        scores = jnp.einsum(
            "iqhe,ikhe->ihqk", projected[0], projected[1], preferred_element_type=jnp.float32
        ) * (1.0 / math.sqrt(DH))
        weights_soft = jax.nn.softmax(scores, axis=-1).astype(jnp.bfloat16)
        attended = (
            jnp.einsum(
                "ihqk,ikhe->iqhe", weights_soft, projected[2], preferred_element_type=jnp.float32
            )
            .astype(jnp.bfloat16)
            .reshape(row_count, head_cols)
        )
        head_terms = jnp.dot(attended, out_weight[0], preferred_element_type=jnp.float32)
        gating_half = mod_half[:, 1][:, None, :]
        summed_half = lax.psum_scatter(
            head_terms.astype(jnp.bfloat16), "tensor", scatter_dimension=1, tiled=True
        ).astype(jnp.float32)
        values_half = hidden_half.reshape(image_count, token_count, half_width)
        result_half = values_half + gating_half * summed_half.reshape(
            image_count, token_count, half_width
        )
        output_half = result_half.reshape(row_count, half_width)
        if tick_index + 1 < TICKS:
            moved_half = from_behind(output_half.astype(jnp.bfloat16), "section", 1).astype(
                output_half.dtype
            )
            moved = lax.all_gather(
                moved_half.astype(jnp.bfloat16), "tensor", axis=1, tiled=True
            ).astype(moved_half.dtype)
            current = jnp.where(section_index == 0, arrivals[tick_index], moved)
    return output_half[None]


def solution(mesh):
    return jax.shard_map(
        on_device,
        mesh=mesh,
        in_specs=(
            P("section", ("groups", "replica"), None),
            P(None, ("groups", "replica"), "section", None),
            P("section", None, "tensor"),
            P("section", None, None, "tensor"),
            P("section", "tensor", None),
            P("section", None, None, "tensor"),
            P(None, "section"),
            P(None, ("groups", "replica")),
        ),
        out_specs=P("section", ("groups", "replica"), "tensor"),
        check_vma=False,
    )
```

profile of v0, /device:TPU:29, one launch (start us, length us, event | category | flops | bytes accessed | tf_op | source)
XLA Modules:
  0.0 218.8 jit_solution(1680848715017906702)
XLA Ops:
  7.4 1.3 copy-done
  8.7 2.4 %fusion.105 = (bf16[256,576]{0,1:T(8,128)(2,1)}, f32[256,576]{0,1:T(8,128)S(1)}) fusion(bf16[1,256,1152]{2,1,0:T(8,128)(2,1)} %param.8, bf16[1,1152,576]{1,2,0:T(8,128)(2,1)S(1)} %copy-done), kind=kOutput, calls=%fused_computation.159 | convolution fusion | flops 339886080 | bytes 2801664 | tf_op jit(solution)/shard_map/dot_general | solution.py:59
  12.3 2.5 %fusion.79 = (s32[]{:T(128)}, s32[]{:T(128)}, s32[]{:T(128)}) fusion(s32[6,1]{0,1:T(1,128)S(1)} %copy-done.10, s32[]{:T(128)} %bitcast.39, s32[]{:T(128)} %bitcast.4, s32[]{:T(128)} %bitcast.24), kind=kLoop, calls=%fused_computation.129 | loop fusion | flops 51 | bytes 48 | tf_op jit(solution)/shard_map/reduce_sum | solution.py:66
  15.5 3.7 %collective-permute-done = bf16[256,576]{0,1:T(8,128)(2,1)} collective-permute-done((bf16[256,576]{0,1:T(8,128)(2,1)}, bf16[256,576]{0,1:T(8,128)(2,1)}, u32[]{:S(2)}, u32[]{:S(2)}) %collective-permute-start) | collective-permute-done | bytes 294944 | tf_op jit(solution)/shard_map/ppermute | solution.py:19
  19.7 3.3 %all-gather.3 = bf16[2,576,2]{1,2,0:T(2,128)(2,1)S(1)} all-gather(bf16[1,576,2]{1,2,0:T(2,128)(2,1)S(1)} %bitcast.201), channel_id=2, replica_groups=mesh['groups'=2,'section'=4,'replica'=2,'tensor'=2] {'tensor'}, dimensions={0}, use_global_device_ids=true | all-gather | bytes 6912 | tf_op jit(solution)/shard_map/all_gather | solution.py:81
  23.2 12.3 %collective-permute-done.1 = bf16[256,576]{0,1:T(8,128)(2,1)S(1)} collective-permute-done((bf16[256,576]{0,1:T(8,128)(2,1)}, bf16[256,576]{0,1:T(8,128)(2,1)S(1)}, u32[]{:S(2)}, u32[]{:S(2)}) %collective-permute-start.1) | collective-permute-done | bytes 294944 | tf_op jit(solution)/shard_map/ppermute | solution.py:19
  36.3 2.5 %all_gather.28 = bf16[256,1152]{0,1:T(8,128)(2,1)S(1)} all-gather(bf16[256,576]{0,1:T(8,128)(2,1)S(1)} %fusion.62), channel_id=1, replica_groups=mesh['groups'=2,'section'=4,'replica'=2,'tensor'=2] {'tensor'}, dimensions={1}, use_global_device_ids=true | all-gather | bytes 884736 | tf_op jit(solution)/shard_map/all_gather | solution.py:78
  39.2 1.1 convolution_convert_fusion.14
  42.6 1.5 fusion.106
  44.2 1.3 convolution_multiply_fusion.2
  45.5 2.7 %convolution_convert_fusion.5 = bf16[4,72,256]{2,1,0:T(8,128)(2,1)} fusion(bf16[256,4,72]{0,2,1:T(8,128)(2,1)} %bitcast.207, f32[4,256]{1,0:T(4,128)S(1)} %fusion.106, f32[4,256,256]{1,2,0:T(8,128)} %convolution_multiply_fusion.2), kind=kOutput, calls=%fused_computation.48 | convolution fusion | flops 38610176 | bytes 1347584 | tf_op jit(solution)/shard_map/ihqk,ikhe->iqhe/dot_general | solution.py:102
  48.2 2.2 %convolution_convert_fusion.2 = bf16[256,1152]{0,1:T(8,128)(2,1)} fusion(bf16[256,288]{0,1:T(8,128)(2,1)} %bitcast.198, bf16[1,288,1152]{2,1,0:T(8,128)(2,1)S(1)} %copy-done.3), kind=kOutput, calls=%fused_computation.5 | convolution fusion | flops 170164224 | bytes 1400832 | tf_op jit(solution)/shard_map/dot_general | solution.py:108
  50.6 2.0 copy.29
  52.6 7.4 %reduce-scatter.4.cloned.1.call-done = bf16[256,576]{0,1:T(8,128)(2,1)} async-done(((bf16[256,1152]{0,1:T(8,128)(2,1)}), bf16[256,576]{0,1:T(8,128)(2,1)}) %reduce-scatter.4.cloned.1.call-update) | async-done | bytes 294928 | tf_op jit(solution)/shard_map/reduce_scatter | solution.py:110
  60.0 2.0 add_convert_fusion.1
  62.0 1.3 collective-permute-start.2
  63.3 25.0 %all-gather.8.cloned.1.call-done = bf16[2,1,256,1152]{3,0,1,2:T(2,128)(2,1)} async-done(((bf16[2,1,64,1152]{3,0,1,2:T(2,128)(2,1)}), bf16[2,1,256,1152]{3,0,1,2:T(2,128)(2,1)}) %all-gather.8.cloned.1.call-update) | async-done | bytes 1179664 | tf_op jit(solution)/shard_map/all_gather | solution.py:46
  88.3 3.5 %copy.30 = bf16[2,1,256,1152]{2,3,1,0:T(8,128)(2,1)S(1)} copy(bf16[2,1,256,1152]{3,0,1,2:T(2,128)(2,1)} %all-gather.8.cloned.1.call-done) | data formatting | bytes 2359296 | tf_op jit(solution)/shard_map/all_gather | solution.py:46
  91.9 2.6 %all_gather.30 = bf16[256,1152]{0,1:T(8,128)(2,1)S(1)} all-gather(bf16[256,576]{0,1:T(8,128)(2,1)} %collective-permute-done.2), channel_id=1, replica_groups=mesh['groups'=2,'section'=4,'replica'=2,'tensor'=2] {'tensor'}, dimensions={1}, use_global_device_ids=true | all-gather | bytes 884736 | tf_op jit(solution)/shard_map/all_gather | solution.py:122
  94.6 1.5 fusion.107
  96.8 7.9 %collective-permute-done.3 = bf16[256,576]{0,1:T(8,128)(2,1)} collective-permute-done((bf16[256,576]{0,1:T(8,128)(2,1)}, bf16[256,576]{0,1:T(8,128)(2,1)}, u32[]{:S(2)}, u32[]{:S(2)}) %collective-permute-start.3) | collective-permute-done | bytes 294944 | tf_op jit(solution)/shard_map/ppermute | solution.py:19
  105.3 3.0 %all-gather.4 = bf16[2,576,2]{1,2,0:T(2,128)(2,1)S(1)} all-gather(bf16[1,576,2]{1,2,0:T(2,128)(2,1)S(1)} %bitcast.202), channel_id=3, replica_groups=mesh['groups'=2,'section'=4,'replica'=2,'tensor'=2] {'tensor'}, dimensions={0}, use_global_device_ids=true | all-gather | bytes 6912 | tf_op jit(solution)/shard_map/all_gather | solution.py:81
  108.4 12.7 %collective-permute-done.4 = bf16[256,576]{0,1:T(8,128)(2,1)} collective-permute-done((bf16[256,576]{0,1:T(8,128)(2,1)}, bf16[256,576]{0,1:T(8,128)(2,1)}, u32[]{:S(2)}, u32[]{:S(2)}) %collective-permute-start.4) | collective-permute-done | bytes 294944 | tf_op jit(solution)/shard_map/ppermute | solution.py:19
  121.1 1.3 fusion.63
  122.4 2.5 %all_gather.31 = bf16[256,1152]{0,1:T(8,128)(2,1)S(1)} all-gather(bf16[256,576]{0,1:T(8,128)(2,1)S(1)} %fusion.63), channel_id=1, replica_groups=mesh['groups'=2,'section'=4,'replica'=2,'tensor'=2] {'tensor'}, dimensions={1}, use_global_device_ids=true | all-gather | bytes 884736 | tf_op jit(solution)/shard_map/all_gather | solution.py:78
  125.3 1.1 convolution_convert_fusion.11
  127.5 1.1 convolution_convert_fusion.9
  128.7 1.5 fusion.108
  130.2 2.3 %convolution_multiply_fusion.1 = f32[4,256,256]{1,2,0:T(8,128)} fusion(bf16[256,4,72]{0,2,1:T(8,128)(2,1)} %bitcast.191, bf16[256,4,72]{0,2,1:T(8,128)(2,1)} %bitcast.193), kind=kOutput, calls=%fused_computation.25 | convolution fusion | flops 38010880 | bytes 1343488 | tf_op jit(solution)/shard_map/iqhe,ikhe->ihqk/dot_general | solution.py:97
  132.5 2.6 %convolution_convert_fusion.4 = bf16[4,72,256]{2,1,0:T(8,128)(2,1)} fusion(bf16[256,4,72]{0,2,1:T(8,128)(2,1)} %bitcast.208, f32[4,256]{1,0:T(4,128)S(1)} %fusion.108, f32[4,256,256]{1,2,0:T(8,128)} %convolution_multiply_fusion.1), kind=kOutput, calls=%fused_computation.47 | convolution fusion | flops 38610176 | bytes 1347584 | tf_op jit(solution)/shard_map/ihqk,ikhe->iqhe/dot_general | solution.py:102
  135.1 2.2 %convolution_convert_fusion.1 = bf16[256,1152]{0,1:T(8,128)(2,1)} fusion(bf16[256,288]{0,1:T(8,128)(2,1)} %bitcast.199, bf16[1,288,1152]{2,1,0:T(8,128)(2,1)S(1)} %copy-done.3), kind=kOutput, calls=%fused_computation.4 | convolution fusion | flops 170164224 | bytes 1400832 | tf_op jit(solution)/shard_map/dot_general | solution.py:108
  137.5 9.4 %reduce-scatter.6.cloned.1.call-done = bf16[256,576]{0,1:T(8,128)(2,1)} async-done(((bf16[256,1152]{0,1:T(8,128)(2,1)}), bf16[256,576]{0,1:T(8,128)(2,1)}) %reduce-scatter.6.cloned.1.call-update) | async-done | bytes 294928 | tf_op jit(solution)/shard_map/reduce_scatter | solution.py:110
  146.9 1.6 add_convert_fusion
  148.5 1.3 collective-permute-start.5
  149.8 9.0 %collective-permute-done.5 = bf16[256,576]{0,1:T(8,128)(2,1)S(1)} collective-permute-done((bf16[256,576]{0,1:T(8,128)(2,1)S(1)}, bf16[256,576]{0,1:T(8,128)(2,1)S(1)}, u32[]{:S(2)}, u32[]{:S(2)}) %collective-permute-start.5) | collective-permute-done | bytes 294944 | tf_op jit(solution)/shard_map/ppermute | solution.py:25
  158.8 2.8 %all_gather.33 = bf16[256,1152]{0,1:T(8,128)(2,1)S(1)} all-gather(bf16[256,576]{0,1:T(8,128)(2,1)S(1)} %collective-permute-done.5), channel_id=1, replica_groups=mesh['groups'=2,'section'=4,'replica'=2,'tensor'=2] {'tensor'}, dimensions={1}, use_global_device_ids=true | all-gather | bytes 884736 | tf_op jit(solution)/shard_map/all_gather | solution.py:122
  161.8 1.5 fusion.109
  164.3 7.5 %collective-permute-done.6 = bf16[256,576]{0,1:T(8,128)(2,1)} collective-permute-done((bf16[256,576]{0,1:T(8,128)(2,1)}, bf16[256,576]{0,1:T(8,128)(2,1)}, u32[]{:S(2)}, u32[]{:S(2)}) %collective-permute-start.6) | collective-permute-done | bytes 294944 | tf_op jit(solution)/shard_map/ppermute | solution.py:19
  172.5 3.0 %all-gather.5 = bf16[2,576,2]{1,2,0:T(2,128)(2,1)S(1)} all-gather(bf16[1,576,2]{1,2,0:T(2,128)(2,1)S(1)} %bitcast.203), channel_id=4, replica_groups=mesh['groups'=2,'section'=4,'replica'=2,'tensor'=2] {'tensor'}, dimensions={0}, use_global_device_ids=true | all-gather | bytes 6912 | tf_op jit(solution)/shard_map/all_gather | solution.py:81
  175.6 12.7 %collective-permute-done.7 = bf16[256,576]{0,1:T(8,128)(2,1)} collective-permute-done((bf16[256,576]{0,1:T(8,128)(2,1)}, bf16[256,576]{0,1:T(8,128)(2,1)}, u32[]{:S(2)}, u32[]{:S(2)}) %collective-permute-start.7) | collective-permute-done | bytes 294944 | tf_op jit(solution)/shard_map/ppermute | solution.py:19
  188.2 1.3 fusion.64
  189.5 2.7 %all_gather.34 = bf16[256,1152]{0,1:T(8,128)(2,1)S(1)} all-gather(bf16[256,576]{0,1:T(8,128)(2,1)S(1)} %fusion.64), channel_id=1, replica_groups=mesh['groups'=2,'section'=4,'replica'=2,'tensor'=2] {'tensor'}, dimensions={1}, use_global_device_ids=true | all-gather | bytes 884736 | tf_op jit(solution)/shard_map/all_gather | solution.py:78
  192.6 1.2 convolution_convert_fusion.8
  195.2 1.3 convolution_multiply_fusion
  196.6 2.0 convolution_convert_fusion.3
  198.6 1.3 convolution_convert_fusion
  199.9 9.5 %reduce-scatter.8.cloned.1.call-done = bf16[256,576]{0,1:T(8,128)(2,1)} async-done(((bf16[256,1152]{0,1:T(8,128)(2,1)}), bf16[256,576]{0,1:T(8,128)(2,1)}) %reduce-scatter.8.cloned.1.call-update) | async-done | bytes 294928 | tf_op jit(solution)/shard_map/reduce_scatter | solution.py:110
  209.5 2.2 %add_bitcast_fusion = f32[1,256,576]{1,2,0:T(8,128)} fusion(bf16[256,576]{0,1:T(8,128)(2,1)} %reduce-scatter.8.cloned.1.call-done, f32[576]{0:T(1024)S(1)} %fusion.71, f32[256,1152]{0,1:T(8,128)S(1)} %fusion.31, s32[]{:T(128)S(6)} %select_n.45, f32[256,576]{0,1:T(8,128)} %get-tuple-element.22, bf16[256,576]{0,1:T(8,128)(2,1)} %collective-permute-done.7, ...), kind=kLoop, calls=%fused_computation.74 | loop fusion | flops 884736 | bytes 2361605 | tf_op jit(solution)/shard_map/add | solution.py:114
  (87 shorter events, 11.5 us)
Async XLA Ops:
  7.4 1.3 copy-start
  7.4 3.9 %copy-start.5 = (bf16[1,256,1152]{2,1,0:T(8,128)(2,1)S(1)}, bf16[1,256,1152]{2,1,0:T(8,128)(2,1)}, u32[]{:S(2)}) copy-start(bf16[1,256,1152]{2,1,0:T(8,128)(2,1)} %param.8) | copy-start | bytes 1769476
  7.4 52.7 %reduce-scatter.4.cloned.1.call-start = ((), (), s32[]{:S(2)}) async-start(), calls=%async_computation.4 | async-start | bytes 884736 | tf_op jit(solution)/shard_map/reduce_scatter | solution.py:110
  11.0 0.7 copy-start.9
  11.0 1.3 copy-start.10
  11.0 8.3 %copy-start.4 = (bf16[1,128,2,576]{1,3,2,0:T(8,128)(2,1)S(1)}, bf16[1,128,2,576]{1,3,2,0:T(8,128)(2,1)}, u32[]{:S(2)}) copy-start(bf16[1,128,2,576]{1,3,2,0:T(8,128)(2,1)} %param.13) | copy-start | bytes 884740
  11.1 8.2 %collective-permute-start = (bf16[256,576]{0,1:T(8,128)(2,1)}, bf16[256,576]{0,1:T(8,128)(2,1)}, u32[]{:S(2)}, u32[]{:S(2)}) collective-permute-start(bf16[256,576]{0,1:T(8,128)(2,1)} %get-tuple-element.17), channel_id=1, source_target_pairs={{0,4},{4,0},{8,12},{12,8},{1,5},{5,1},{9,13},{13,9},{2,6},{6,2},{1... | collective-permute-start | bytes 884744 | tf_op jit(solution)/shard_map/ppermute | solution.py:19
  19.2 16.3 %collective-permute-start.1 = (bf16[256,576]{0,1:T(8,128)(2,1)}, bf16[256,576]{0,1:T(8,128)(2,1)S(1)}, u32[]{:S(2)}, u32[]{:S(2)}) collective-permute-start(bf16[256,576]{0,1:T(8,128)(2,1)} %collective-permute-done), channel_id=1, source_target_pairs={{0,8},{4,12},{8,0},{12,4},{1,9},{5,13},{9,1},{13,5},{2,10},{6,14},... | collective-permute-start | bytes 884744 | tf_op jit(solution)/shard_map/ppermute | solution.py:19
  35.5 0.7 copy-start.6
  36.3 2.9 %copy-start.11 = (bf16[1,3,1152,288]{2,3,1,0:T(8,128)(2,1)S(1)}, bf16[1,3,1152,288]{2,3,1,0:T(8,128)(2,1)}, u32[]{:S(2)}) copy-start(bf16[1,3,1152,288]{2,3,1,0:T(8,128)(2,1)} %param.11) | copy-start | bytes 5971972
  42.6 1.6 copy-start.7
  42.6 1.6 copy-start.8
  45.5 2.7 %copy-start.3 = (bf16[1,288,1152]{2,1,0:T(8,128)(2,1)S(1)}, bf16[1,288,1152]{2,1,0:T(8,128)(2,1)}, u32[]{:S(2)}) copy-start(bf16[1,288,1152]{2,1,0:T(8,128)(2,1)} %param.12) | copy-start | bytes 1990660
  50.5 37.8 %all-gather.8.cloned.1.call-start = ((), (), s32[]{:S(2)}) async-start(), calls=%async_computation.3 | async-start | bytes 1474560 | tf_op jit(solution)/shard_map/all_gather | solution.py:46
  52.6 94.4 %reduce-scatter.6.cloned.1.call-start = ((), (), s32[]{:S(2)}) async-start(), calls=%async_computation.5 | async-start | bytes 884736 | tf_op jit(solution)/shard_map/reduce_scatter | solution.py:110
  62.0 29.9 %collective-permute-start.2 = (bf16[256,576]{0,1:T(8,128)(2,1)}, bf16[256,576]{0,1:T(8,128)(2,1)}, u32[]{:S(2)}, u32[]{:S(2)}) collective-permute-start(bf16[256,576]{0,1:T(8,128)(2,1)} %add_convert_fusion.1), channel_id=1, source_target_pairs={{0,4},{4,8},{8,12},{1,5},{5,9},{9,13},{2,6},{6,10},{10,14},{3,7},{... | collective-permute-start | bytes 884744 | tf_op jit(solution)/shard_map/ppermute | solution.py:25
  91.9 2.7 %copy-start.1 = (f32[2,1,256,1152]{2,3,1,0:T(8,128)}, f32[2,1,256,1152]{2,3,1,0:T(8,128)S(1)}, u32[]{:S(2)}) copy-start(f32[2,1,256,1152]{2,3,1,0:T(8,128)S(1)} %convert_element_type.213) | copy-start | bytes 7077892
  96.1 8.5 %collective-permute-start.3 = (bf16[256,576]{0,1:T(8,128)(2,1)}, bf16[256,576]{0,1:T(8,128)(2,1)}, u32[]{:S(2)}, u32[]{:S(2)}) collective-permute-start(bf16[256,576]{0,1:T(8,128)(2,1)} %get-tuple-element.19), channel_id=1, source_target_pairs={{0,4},{4,0},{8,12},{12,8},{1,5},{5,1},{9,13},{13,9},{2,6},{6,2},{1... | collective-permute-start | bytes 884744 | tf_op jit(solution)/shard_map/ppermute | solution.py:19
  104.7 16.4 %collective-permute-start.4 = (bf16[256,576]{0,1:T(8,128)(2,1)}, bf16[256,576]{0,1:T(8,128)(2,1)}, u32[]{:S(2)}, u32[]{:S(2)}) collective-permute-start(bf16[256,576]{0,1:T(8,128)(2,1)} %collective-permute-done.3), channel_id=1, source_target_pairs={{0,8},{4,12},{8,0},{12,4},{1,9},{5,13},{9,1},{13,5},{2,10},{6,14},... | collective-permute-start | bytes 884744 | tf_op jit(solution)/shard_map/ppermute | solution.py:19
  122.4 2.9 %copy-start.12 = (bf16[1,3,1152,288]{2,3,1,0:T(8,128)(2,1)S(1)}, bf16[1,3,1152,288]{2,3,1,0:T(8,128)(2,1)}, u32[]{:S(2)}) copy-start(bf16[1,3,1152,288]{2,3,1,0:T(8,128)(2,1)} %param.11) | copy-start | bytes 5971972
  137.4 72.1 %reduce-scatter.8.cloned.1.call-start = ((), (), s32[]{:S(2)}) async-start(), calls=%async_computation.6 | async-start | bytes 884736 | tf_op jit(solution)/shard_map/reduce_scatter | solution.py:110
  146.9 14.7 %copy-start.2 = (f32[2,1,256,1152]{2,3,1,0:T(8,128)S(1)}, f32[2,1,256,1152]{2,3,1,0:T(8,128)}, u32[]{:S(2)}) copy-start(f32[2,1,256,1152]{2,3,1,0:T(8,128)} %copy-done.1) | copy-start | bytes 7077892
  148.5 10.3 %collective-permute-start.5 = (bf16[256,576]{0,1:T(8,128)(2,1)S(1)}, bf16[256,576]{0,1:T(8,128)(2,1)S(1)}, u32[]{:S(2)}, u32[]{:S(2)}) collective-permute-start(bf16[256,576]{0,1:T(8,128)(2,1)S(1)} %add_convert_fusion), channel_id=1, source_target_pairs={{0,4},{4,8},{8,12},{1,5},{5,9},{9,13},{2,6},{6,10},{10,14},{3,7},{... | collective-permute-start | bytes 884744 | tf_op jit(solution)/shard_map/ppermute | solution.py:25
  163.3 8.5 %collective-permute-start.6 = (bf16[256,576]{0,1:T(8,128)(2,1)}, bf16[256,576]{0,1:T(8,128)(2,1)}, u32[]{:S(2)}, u32[]{:S(2)}) collective-permute-start(bf16[256,576]{0,1:T(8,128)(2,1)} %get-tuple-element.21), channel_id=1, source_target_pairs={{0,4},{4,0},{8,12},{12,8},{1,5},{5,1},{9,13},{13,9},{2,6},{6,2},{1... | collective-permute-start | bytes 884744 | tf_op jit(solution)/shard_map/ppermute | solution.py:19
  171.8 16.4 %collective-permute-start.7 = (bf16[256,576]{0,1:T(8,128)(2,1)}, bf16[256,576]{0,1:T(8,128)(2,1)}, u32[]{:S(2)}, u32[]{:S(2)}) collective-permute-start(bf16[256,576]{0,1:T(8,128)(2,1)} %collective-permute-done.6), channel_id=1, source_target_pairs={{0,8},{4,12},{8,0},{12,4},{1,9},{5,13},{9,1},{13,5},{2,10},{6,14},... | collective-permute-start | bytes 884744 | tf_op jit(solution)/shard_map/ppermute | solution.py:19
  189.5 3.1 %copy-start.13 = (bf16[1,3,1152,288]{2,3,1,0:T(8,128)(2,1)S(1)}, bf16[1,3,1152,288]{2,3,1,0:T(8,128)(2,1)}, u32[]{:S(2)}) copy-start(bf16[1,3,1152,288]{2,3,1,0:T(8,128)(2,1)} %param.11) | copy-start | bytes 5971972
Sparse Core Ops, SparseCore 0:
  50.6 9.3 reduce-scatter.3
  137.5 9.3 reduce-scatter.5
  200.0 9.3 reduce-scatter.7
Sparse Core Ops, SparseCore 1:
  52.6 35.6 all-gather.7
where the time goes:
time: 221 us; the launch traced here: 219 us
  waiting for transfers between devices  117 us (53%)
  matrix products  37.2 us (17%)
  blocking collectives  22.3 us (10%)
  between operations  16.7 us (8%)
  other arithmetic  12.8 us (6%)
  local copies, waits for them, and re-layouts  8.91 us (4%)
  starting transfers between devices  3.67 us (2%)
    ppermute x6, waiting for transfers between devices, swapped(): return lax.ppermute(value, axis, pairs)  56.8 us
    reduce_scatter x3, waiting for transfers between devices, on_device(): lax.psum_scatter(head_terms.astype(jnp.bfloat16), 'tensor', scatter_dimen...  26.4 us
    all_gather x1, waiting for transfers between devices, on_device(): arrivals = lax.all_gather(fresh_rows, 'section', axis=2, tiled=True)  25 us
    all_gather x3, blocking collectives, on_device(): lax.all_gather(mod_half.astype(jnp.bfloat16), 'tensor', axis=2, tiled=True)  9.25 us
    ppermute x2, waiting for transfers between devices, from_behind(): lax.ppermute(value, axis, [(source, source + steps) for source in range(i...  9.04 us
    dot_general x9, matrix products, on_device(): jnp.dot(mixed, qkv_weight[0, index], preferred_element_type=jnp.float32)  8.92 us
    all_gather x3, blocking collectives, on_device(): lax.all_gather(hidden_half.astype(jnp.bfloat16), 'tensor', axis=1, tiled=...  7.62 us
    dot_general x3, matrix products, on_device(): jnp.einsum('ihqk,ikhe->iqhe', weights_soft, projected[2], preferred_eleme...  7.33 us
  transfers between devices with their start and end apart: 12, of which 11 were waited for; matrix products, arithmetic and copies ran while one was open for 6% of the time, Pallas kernels for 0%

commit v1 on v0

v1 whole, which is shorter than its diff:
```python
import functools
import math

import jax
import jax.numpy as jnp
from jax import lax
from jax.experimental import pallas as pl
from jax.experimental.pallas import tpu as pltpu
from jax.sharding import PartitionSpec as P

DH = 72
FREQ = 128
TICKS = 3
epsilon = 1e-06
F32 = jnp.float32
BF16 = jnp.bfloat16


def timestep_embed(times):
    half_width = FREQ // 2
    frequency = jnp.exp(-math.log(10000.0) * jnp.arange(half_width, dtype=F32) / half_width)
    phases = times.astype(F32)[:, None] * frequency[None, :]
    return jnp.concatenate([jnp.cos(phases), jnp.sin(phases)], axis=1)


def dot(a, b):
    return jnp.dot(a, b, preferred_element_type=F32)


def kernel(
    sections,
    inflow_ref,
    fresh_ref,
    lin_ref,
    qkv_ref,
    out_w_ref,
    mod_ref,
    out_ref,
    lin_other,
    lin_full,
    out_split,
    mod_other,
    mod_full,
    fresh_in,
    xin,
    skip_out,
    skip_in,
    hidden,
    u_buf,
    q_buf,
    k_buf,
    v_buf,
    g_out,
    g_in,
    gl_out,
    gl_in,
    h_cols,
    h_in,
    y_out,
    lin_sem,
    mod_sem,
    fresh_send,
    fresh_recv,
    x_send,
    x_recv,
    skip_send,
    skip_recv,
    u_send,
    u_recv,
    g_send,
    g_recv,
    gl_send,
    gl_recv,
    h_sem,
):
    s = lax.axis_index("section")
    c = lax.axis_index("tensor")
    o = 1 - c
    half = sections // 2
    mirror = sections - 1 - s
    down = s < half
    rows = inflow_ref.shape[1]
    width = inflow_ref.shape[2]
    half_width = width // 2
    heads = out_w_ref.shape[0] // DH
    head_cols = out_w_ref.shape[0]
    last = TICKS - 1

    def remote(src, dst, send, recv, device):
        return pltpu.make_async_remote_copy(
            src_ref=src,
            dst_ref=dst,
            send_sem=send,
            recv_sem=recv,
            device_id=device,
            device_id_type=pl.DeviceIdType.MESH,
        )

    fresh_sender = (s > 0) & (s // half == c)

    barrier = pltpu.get_barrier_semaphore()

    def greet(device):
        pl.semaphore_signal(
            barrier, inc=1, device_id=device, device_id_type=pl.DeviceIdType.MESH
        )

    greet({"tensor": o})
    greet({"section": mirror})

    @pl.when(s > 0)
    def _():
        greet({"section": s - 1})

    @pl.when(s < sections - 1)
    def _():
        greet({"section": s + 1})

    @pl.when(fresh_sender)
    def _():
        greet({"section": 0})

    @pl.when(s == 0)
    def _():
        for block in range(half):

            @pl.when((c * half + block) > 0)
            def _():
                greet({"section": c * half + block})

    expected = (
        2
        + jnp.where(s > 0, 1, 0)
        + jnp.where(s < sections - 1, 1, 0)
        + jnp.where(fresh_sender, 1, 0)
        + jnp.where(s == 0, half - 1 + c, 0)
    )
    pl.semaphore_wait(barrier, expected)

    def fresh_copy(tick, block):
        return remote(
            fresh_ref.at[tick],
            fresh_in.at[tick, block],
            fresh_send.at[tick],
            fresh_recv.at[tick, block],
            {"section": 0},
        )

    @pl.when(fresh_sender)
    def _():
        for tick in range(TICKS - 1):
            fresh_copy(tick, s % half).start()

    lin_copy = remote(lin_ref, lin_other, lin_sem.at[0], lin_sem.at[1], {"tensor": o})
    mod_copy = remote(mod_ref, mod_other, mod_sem.at[0], mod_sem.at[1], {"tensor": o})
    mod_copy.start()

    out_split[0] = out_w_ref[:, :half_width]
    out_split[1] = out_w_ref[:, half_width:]
    xin[0] = inflow_ref[c]
    mod_copy.wait()

    @pl.when(c == 0)
    def _():
        mod_full[...] = jnp.concatenate([mod_ref[...], mod_other[...]], axis=1)

    @pl.when(c == 1)
    def _():
        mod_full[...] = jnp.concatenate([mod_other[...], mod_ref[...]], axis=1)

    def skip_copy(tick):
        return remote(
            skip_out.at[tick],
            skip_in.at[tick],
            skip_send.at[tick],
            skip_recv.at[tick],
            {"section": mirror},
        )

    def x_copy(tick):
        return remote(
            y_out.at[tick],
            xin.at[tick + 1],
            x_send.at[tick],
            x_recv.at[tick],
            {"section": s + 1},
        )

    def x_wait(tick):
        remote(
            y_out.at[tick],
            xin.at[tick + 1],
            x_send.at[tick],
            x_recv.at[tick],
            {"section": s - 1},
        ).wait_recv()

    def linear(tick):
        return dot(xin[tick], lin_full[...])

    def fresh_arrive(tick):
        for block in range(half):

            @pl.when((c * half + block) > 0)
            def _():
                remote(
                    fresh_ref.at[tick],
                    fresh_in.at[tick, block],
                    fresh_send.at[tick],
                    fresh_recv.at[tick, block],
                    {"section": c * half + block},
                ).wait_recv()

        @pl.when(c == 0)
        def _():
            fresh_in[tick, 0] = fresh_ref[tick]

        xin[tick + 1] = fresh_in[tick].astype(F32).reshape(rows, width).astype(BF16)

    lane_head = lax.broadcasted_iota(jnp.int32, (rows, head_cols), 1)
    head_masks = [(lane_head >= DH * h) & (lane_head < DH * (h + 1)) for h in range(heads)]
    scale = 1.0 / math.sqrt(DH)

    def attend(part):
        q = q_buf[part]
        k = k_buf[...].reshape(2 * rows, head_cols)
        v = v_buf[...].reshape(2 * rows, head_cols)
        total = None
        for h in range(heads):
            q_h = jnp.where(head_masks[h], q, jnp.zeros_like(q))
            scores = (
                lax.dot_general(q_h, k, (((1,), (1,)), ((), ())), preferred_element_type=F32)
                * scale
            )
            top = jnp.max(scores, axis=-1, keepdims=True)
            grown = jnp.exp(scores - top)
            soft = (grown / jnp.sum(grown, axis=-1, keepdims=True)).astype(BF16)
            product = dot(soft, v)
            total = product if h == 0 else jnp.where(head_masks[h], product, total)
        return total.astype(BF16)

    def u_copy(tick):
        return remote(
            u_buf.at[tick, c], u_buf.at[tick, c], u_send.at[tick], u_recv.at[tick], {"tensor": o}
        )

    def u_wait(tick):
        remote(
            u_buf.at[tick, o], u_buf.at[tick, o], u_send.at[tick], u_recv.at[tick], {"tensor": o}
        ).wait_recv()

    def project(tick, part):
        rows_in = u_buf[tick, part]
        q_buf[part] = dot(rows_in, qkv_ref[0]).astype(BF16)
        k_buf[part] = dot(rows_in, qkv_ref[1]).astype(BF16)
        v_buf[part] = dot(rows_in, qkv_ref[2]).astype(BF16)

    def h_copy():
        return remote(h_cols.at[o], h_in, h_sem.at[0], h_sem.at[1], {"tensor": o})

    def block(tick):
        values = hidden[...]
        centred = values - jnp.mean(values, axis=-1, keepdims=True)
        variance = jnp.mean(centred * centred, axis=-1, keepdims=True)
        normed = centred * lax.rsqrt(variance + epsilon)
        scaling = mod_full[2 * tick : 2 * tick + 1, :]
        u_buf[tick, c] = (normed * (1.0 + scaling)).astype(BF16)
        u_copy(tick).start()
        project(tick, c)
        if tick == last:
            h_cols[0] = hidden[:, :half_width]
            h_cols[1] = hidden[:, half_width:]
            h_copy().start()
        u_wait(tick)
        project(tick, o)

    def g_copy(tick):
        return remote(
            g_out.at[tick], g_in.at[tick], g_send.at[tick], g_recv.at[tick], {"tensor": o}
        )

    def relay(tick):
        g_out[tick] = dot(attend(o), out_w_ref[...]).astype(BF16)
        g_copy(tick).start()
        own = dot(attend(c), out_w_ref[...]).astype(BF16).astype(F32)
        gating = mod_full[2 * tick + 1 : 2 * tick + 2, :]
        g_copy(tick).wait_recv()
        y = hidden[...] + gating * (own + g_in[tick].astype(F32))
        y_out[tick] = y.astype(BF16)
        x_copy(tick).start()

    def gl_copy(part):
        return remote(
            gl_out.at[part], gl_in.at[part], gl_send.at[part], gl_recv.at[part], {"tensor": o}
        )

    def settle():
        gating = mod_ref[2 * last + 1 : 2 * last + 2, :]
        for part in range(2):
            heads_out = attend(part)
            gl_out[part] = dot(heads_out, out_split[o]).astype(BF16)
            gl_copy(part).start()
            out_ref[part] = dot(heads_out, out_split[c]).astype(BF16).astype(F32)
        h_copy().wait_recv()
        for part in range(2):
            gl_copy(part).wait_recv()
            summed = out_ref[part] + gl_in[part].astype(F32)
            h_part = jnp.where(c == part, h_cols[c], h_in[...])
            out_ref[part] = h_part + gating * summed

    def skip_needed(tick):
        return down & (mirror <= sections - TICKS + tick)

    def send_skip(tick):
        skip_out[tick] = linear(tick).astype(BF16)
        skip_copy(tick).start()

    lin_copy.start()

    for tick in range(TICKS):
        live = s <= sections - TICKS + tick

        @pl.when((s > 0) & live)
        def _():
            if tick > 0:
                x_wait(tick - 1)

        def prepare_linear():
            lin_copy.wait()

            @pl.when(c == 0)
            def _():
                lin_full[...] = jnp.concatenate([lin_ref[...], lin_other[...]], axis=1)

            @pl.when(c == 1)
            def _():
                lin_full[...] = jnp.concatenate([lin_other[...], lin_ref[...]], axis=1)

        if tick == 0:
            first_linear = skip_needed(0) | (jnp.logical_not(down))

            @pl.when(first_linear)
            def _():
                prepare_linear()

        if tick > 0:

            @pl.when(skip_needed(tick) & (s > 0))
            def _():
                send_skip(tick)

        else:

            @pl.when(skip_needed(tick))
            def _():
                send_skip(tick)

        @pl.when(live & down)
        def _():
            hidden[...] = xin[tick].astype(F32)

        @pl.when(live & jnp.logical_not(down))
        def _():
            own = linear(tick)
            remote(
                skip_out.at[tick],
                skip_in.at[tick],
                skip_send.at[tick],
                skip_recv.at[tick],
                {"section": mirror},
            ).wait_recv()
            hidden[...] = own + skip_in[tick].astype(F32)

        if tick < last:

            @pl.when(live)
            def _():
                block(tick)
                relay(tick)

        else:
            block(tick)
            settle()

        if tick == 0:

            @pl.when(jnp.logical_not(first_linear))
            def _():
                prepare_linear()

            @pl.when(s == 0)
            def _():
                for later in range(TICKS - 1):
                    fresh_arrive(later)
                for later in range(1, TICKS):

                    @pl.when(skip_needed(later))
                    def _():
                        send_skip(later)

    @pl.when(fresh_sender)
    def _():
        for tick in range(TICKS - 1):
            fresh_copy(tick, s % half).wait_send()

    h_copy().wait_send()
    for part in range(2):
        gl_copy(part).wait_send()
    for tick in range(TICKS):

        @pl.when(skip_needed(tick))
        def _():
            skip_copy(tick).wait_send()

        @pl.when(s <= sections - TICKS + tick)
        def _():
            u_copy(tick).wait_send()
            if tick < last:
                g_copy(tick).wait_send()
                x_copy(tick).wait_send()


def on_device(inflow, fresh_rows, lin_weight, qkv_weight, out_weight, mod_weight, plan, timesteps):
    sections = lax.axis_size("section")
    row_count, width = inflow.shape[1:]
    rows = row_count // 2
    half_width = lin_weight.shape[2]
    head_cols = out_weight.shape[1]
    half = sections // 2
    piece = fresh_rows.shape[2]
    micro_ids = lax.broadcasted_iota(jnp.int32, (TICKS, timesteps.shape[0]), 1)
    times = jnp.sum(jnp.where(micro_ids == plan, timesteps[:, 0][None, :], 0), axis=1)
    modulation = (
        jnp.einsum(
            "tf,fcd->tcd",
            timestep_embed(times),
            mod_weight[0].astype(F32),
            precision=lax.Precision.HIGHEST,
        )
        .astype(BF16)
        .astype(F32)
        .reshape(2 * TICKS, half_width)
    )
    modulation = jnp.pad(modulation, ((0, 8 - 2 * TICKS), (0, 0)))
    vmem = pl.BlockSpec(memory_space=pltpu.VMEM)
    dma = pltpu.SemaphoreType.DMA
    settled = pl.pallas_call(
        functools.partial(kernel, sections),
        out_shape=jax.ShapeDtypeStruct((2, rows, half_width), F32),
        in_specs=[vmem] * 6,
        out_specs=vmem,
        scratch_shapes=[
            pltpu.VMEM((width, half_width), BF16),
            pltpu.VMEM((width, width), BF16),
            pltpu.VMEM((2, head_cols, half_width), BF16),
            pltpu.VMEM((8, half_width), F32),
            pltpu.VMEM((8, width), F32),
            pltpu.VMEM((TICKS - 1, half, piece, width), BF16),
            pltpu.VMEM((TICKS, rows, width), BF16),
            pltpu.VMEM((TICKS, rows, width), BF16),
            pltpu.VMEM((TICKS, rows, width), BF16),
            pltpu.VMEM((rows, width), F32),
            pltpu.VMEM((TICKS, 2, rows, width), BF16),
            pltpu.VMEM((2, rows, head_cols), BF16),
            pltpu.VMEM((2, rows, head_cols), BF16),
            pltpu.VMEM((2, rows, head_cols), BF16),
            pltpu.VMEM((TICKS - 1, rows, width), BF16),
            pltpu.VMEM((TICKS - 1, rows, width), BF16),
            pltpu.VMEM((2, rows, half_width), BF16),
            pltpu.VMEM((2, rows, half_width), BF16),
            pltpu.VMEM((2, rows, half_width), F32),
            pltpu.VMEM((rows, half_width), F32),
            pltpu.VMEM((TICKS - 1, rows, width), BF16),
            dma((2,)),
            dma((2,)),
            dma((TICKS - 1,)),
            dma((TICKS - 1, half)),
            dma((TICKS - 1,)),
            dma((TICKS - 1,)),
            dma((TICKS,)),
            dma((TICKS,)),
            dma((TICKS,)),
            dma((TICKS,)),
            dma((TICKS - 1,)),
            dma((TICKS - 1,)),
            dma((2,)),
            dma((2,)),
            dma((2,)),
        ],
        compiler_params=pltpu.CompilerParams(
            collective_id=0, has_side_effects=True, vmem_limit_bytes=44 * 2**20
        ),
    )(
        inflow[0].reshape(2, rows, width),
        fresh_rows[:, 0],
        lin_weight[0],
        qkv_weight[0],
        out_weight[0],
        modulation,
    )
    return settled.reshape(1, row_count, half_width)


def solution(mesh):
    return jax.shard_map(
        on_device,
        mesh=mesh,
        in_specs=(
            P("section", ("groups", "replica"), None),
            P(None, ("groups", "replica"), "section", None),
            P("section", None, "tensor"),
            P("section", None, None, "tensor"),
            P("section", "tensor", None),
            P("section", None, None, "tensor"),
            P(None, "section"),
            P(None, ("groups", "replica")),
        ),
        out_specs=P("section", ("groups", "replica"), "tensor"),
        check_vma=False,
    )
```

time: 221 us -> 72.6 us (0.33)
  waiting for transfers between devices: 117 us -> 0 us
  Pallas kernels: 0 us -> 57.2 us
  matrix products: 37.2 us -> 0.43 us
  blocking collectives: 22.3 us -> 0 us
  between operations: 16.7 us -> 0.07 us
  other arithmetic: 12.8 us -> 1.64 us
  local copies, waits for them, and re-layouts: 8.91 us -> 12.8 us
  starting transfers between devices: 3.67 us -> 0 us
    ppermute x8 -> x0, waiting for transfers between devices: 65.9 us -> none  [the longest x6 56.8 us: swapped(): return lax.ppermute(value, axis, pairs)]
    pallas_call x0 -> x1, Pallas kernels: none -> 57.2 us  [on_device(): pl.pallas_call(functools.partial(kernel, sections), out_shape=jax.ShapeDt...]
    dot_general x24 -> x1, matrix products: 33.6 us -> 0.43 us  [on_device(): jnp.einsum('tf,fcd->tcd', timestep_embed(times), mod_weight[0].astype(F32...]
    reduce_scatter x3 -> x0, waiting for transfers between devices: 26.4 us -> none  [on_device(): lax.psum_scatter(head_terms.astype(jnp.bfloat16), 'tensor', scatter_dimen...]
    all_gather x1 -> x0, waiting for transfers between devices: 25 us -> none  [on_device(): arrivals = lax.all_gather(fresh_rows, 'section', axis=2, tiled=True)]
    all_gather x8 -> x0, blocking collectives: 22.3 us -> none  [the longest x3 9.25 us: on_device(): lax.all_gather(mod_half.astype(jnp.bfloat16), 'tensor', axis=2, tiled=True)]
    convert_element_type x6 -> x1, other arithmetic: 6.41 us -> 0.01 us  [timestep_embed(): phases = times.astype(F32)[:, None] * frequency[None, :]]
    unnamed x33 -> x16, local copies, waits for them, and re-layouts: 4.81 us -> 10.7 us
  transfers between devices with their start and end apart: 12 -> 0, of which waited for: 11 -> 0; matrix products, arithmetic and copies ran while one was open for 6% -> 0% of each run, Pallas kernels for 0% -> 0%
where the time goes in v1:
time: 72.6 us; the launch traced here: 72.2 us
  Pallas kernels  57.2 us (79%)
  local copies, waits for them, and re-layouts  12.8 us (18%)
  other arithmetic  1.64 us (2%)
    pallas_call x1, Pallas kernels, on_device(): pl.pallas_call(functools.partial(kernel, sections), out_shape=jax.ShapeDt...  57.2 us
    unnamed x16, local copies, waits for them, and re-layouts  10.7 us
    reshape x1, local copies, waits for them, and re-layouts, on_device(): return settled.reshape(1, row_count, half_width)  2.12 us

profile of v1, /device:TPU:29, one launch (start us, length us, event | category | flops | bytes accessed | tf_op | source)
XLA Modules:
  0.0 72.2 jit_solution(5592683816524121758)
XLA Ops:
  0.0 0.0 copy-start
  0.0 0.9 %select_reduce_fusion = s32[3]{0:T(128)S(1)} fusion(s32[6]{0:T(128)} %bitcast.20, s32[3]{0:T(128)} %bitcast.21), kind=kLoop, calls=%fused_computation.8 | loop fusion | flops 51 | bytes 48 | tf_op jit(solution)/shard_map/reduce_sum | solution.py:432
  0.9 0.1 multiply_cosine_fusion
  1.0 0.0 copy-done
  1.0 0.4 convolution_convert_fusion
  1.5 0.6 pad_convert_fusion.mod_ref
  2.1 2.6 %copy.13 = bf16[1,1152,576]{2,1,0:T(8,128)(2,1)} copy(bf16[1,1152,576]{1,2,0:T(8,128)(2,1)} %param.10) | data formatting | bytes 2654208 | tf_op args[2]
  4.8 0.0 copy-start.4
  4.8 3.1 %copy.14 = bf16[1,3,1152,288]{3,2,1,0:T(8,128)(2,1)S(1)} copy(bf16[1,3,1152,288]{2,3,1,0:T(8,128)(2,1)} %param.11) | data formatting | bytes 3981312 | tf_op args[3]
  7.8 0.0 copy-done.4
  7.8 0.0 copy-start.1
  7.9 1.4 %copy-done.1 = bf16[1,1152,576]{2,1,0:T(8,128)(2,1)S(1)} copy-done((bf16[1,1152,576]{2,1,0:T(8,128)(2,1)S(1)}, bf16[1,1152,576]{2,1,0:T(8,128)(2,1)}, u32[]{:S(2)}) %copy-start.1) | copy-done | bytes 1327128
  9.2 0.0 copy-start.3
  9.2 1.1 %copy-done.3 = bf16[1,288,1152]{2,1,0:T(8,128)(2,1)S(1)} copy-done((bf16[1,288,1152]{2,1,0:T(8,128)(2,1)S(1)}, bf16[1,288,1152]{2,1,0:T(8,128)(2,1)}, u32[]{:S(2)}) %copy-start.3) | copy-done | bytes 663576
  10.3 0.0 copy-start.5
  10.3 1.0 %copy-done.5 = bf16[2,1,64,1152]{3,2,1,0:T(8,128)(2,1)S(1)} copy-done((bf16[2,1,64,1152]{3,2,1,0:T(8,128)(2,1)S(1)}, bf16[2,1,64,1152]{3,2,1,0:T(8,128)(2,1)}, u32[]{:S(2)}) %copy-start.5) | copy-done | bytes 294936
  11.3 0.0 copy-start.6
  11.3 0.7 %copy-done.6 = f32[8,576]{1,0:T(8,128)S(1)} copy-done((f32[8,576]{1,0:T(8,128)S(1)}, f32[8,576]{1,0:T(8,128)}, u32[]{:S(2)}) %copy-start.6) | copy-done | bytes 18456
  12.0 57.2 %shard_map.82 = f32[2,128,576]{2,1,0:T(8,128)S(1)} custom-call(bf16[2,128,1152]{2,1,0:T(8,128)(2,1)S(1)} %bitcast.18, bf16[2,64,1152]{2,1,0:T(8,128)(2,1)S(1)} %bitcast.19, bf16[1152,576]{1,0:T(8,128)(2,1)S(1)} %bitcast.15, bf16[3,1152,288]{2,1,0:T(8,128)(2,1)S(1)} %bitcast.14, bf16[288,1152]{1,0:T(8,128)(2,1)S(1)} %bitcast.17, f32[8,576]{1,0:T(8,128)S(1)} %copy-done.6), custom_call_target="tpu_custom_call" | custom-call | tf_op jit(solution)/shard_map/pallas_call | solution.py:447
  69.2 0.0 copy-start.2
  69.2 0.8 %copy-done.2 = f32[2,128,576]{2,1,0:T(8,128)} copy-done((f32[2,128,576]{2,1,0:T(8,128)}, f32[2,128,576]{2,1,0:T(8,128)S(1)}, u32[]{:S(2)}) %copy-start.2) | copy-done | bytes 589848
  70.1 2.1 %copy.16 = f32[1,256,576]{1,2,0:T(8,128)} copy(f32[1,256,576]{2,1,0:T(8,128)} %bitcast.16) | data formatting | bytes 1179648 | tf_op jit(solution)/shard_map/reshape | solution.py:501
  (4 shorter events, 0.1 us)
Async XLA Ops:
  0.0 1.0 %copy-start = (bf16[1,128,2,576]{1,3,2,0:T(8,128)(2,1)S(1)}, bf16[1,128,2,576]{1,3,2,0:T(8,128)(2,1)}, u32[]{:S(2)}) copy-start(bf16[1,128,2,576]{1,3,2,0:T(8,128)(2,1)} %param.13) | copy-start | bytes 884740
  4.8 3.1 %copy-start.4 = (bf16[1,256,1152]{2,1,0:T(8,128)(2,1)S(1)}, bf16[1,256,1152]{2,1,0:T(8,128)(2,1)}, u32[]{:S(2)}) copy-start(bf16[1,256,1152]{2,1,0:T(8,128)(2,1)} %param.8) | copy-start | bytes 1769476
  7.8 1.4 %copy-start.1 = (bf16[1,1152,576]{2,1,0:T(8,128)(2,1)S(1)}, bf16[1,1152,576]{2,1,0:T(8,128)(2,1)}, u32[]{:S(2)}) copy-start(bf16[1,1152,576]{2,1,0:T(8,128)(2,1)} %copy.13) | copy-start | bytes 3981316
  9.2 1.1 %copy-start.3 = (bf16[1,288,1152]{2,1,0:T(8,128)(2,1)S(1)}, bf16[1,288,1152]{2,1,0:T(8,128)(2,1)}, u32[]{:S(2)}) copy-start(bf16[1,288,1152]{2,1,0:T(8,128)(2,1)} %param.12) | copy-start | bytes 1990660
  10.3 1.0 %copy-start.5 = (bf16[2,1,64,1152]{3,2,1,0:T(8,128)(2,1)S(1)}, bf16[2,1,64,1152]{3,2,1,0:T(8,128)(2,1)}, u32[]{:S(2)}) copy-start(bf16[2,1,64,1152]{3,2,1,0:T(8,128)(2,1)} %param.9) | copy-start | bytes 884740
  11.3 0.7 %copy-start.6 = (f32[8,576]{1,0:T(8,128)S(1)}, f32[8,576]{1,0:T(8,128)}, u32[]{:S(2)}) copy-start(f32[8,576]{1,0:T(8,128)} %pad_convert_fusion.mod_ref) | copy-start | bytes 55300
  69.2 0.8 %copy-start.2 = (f32[2,128,576]{2,1,0:T(8,128)}, f32[2,128,576]{2,1,0:T(8,128)S(1)}, u32[]{:S(2)}) copy-start(f32[2,128,576]{2,1,0:T(8,128)S(1)} %shard_map.82) | copy-start | bytes 1769476

commit v2 on v1

--- a/solution.py
+++ b/solution.py
@@ -16,31 +16,34 @@
 BF16 = jnp.bfloat16
 
 
-def timestep_embed(times):
-    half_width = FREQ // 2
-    frequency = jnp.exp(-math.log(10000.0) * jnp.arange(half_width, dtype=F32) / half_width)
-    phases = times.astype(F32)[:, None] * frequency[None, :]
-    return jnp.concatenate([jnp.cos(phases), jnp.sin(phases)], axis=1)
-
-
 def dot(a, b):
     return jnp.dot(a, b, preferred_element_type=F32)
 
 
+def dot_t(a, b):
+    return lax.dot_general(a, b, (((1,), (1,)), ((), ())), preferred_element_type=F32)
+
+
 def kernel(
     sections,
-    inflow_ref,
+    inflow_hbm,
     fresh_ref,
     lin_ref,
+    qkv_hbm,
+    out_w_hbm,
+    mod_hbm,
+    plan_ref,
+    times_ref,
+    out_ref,
     qkv_ref,
     out_w_ref,
-    mod_ref,
-    out_ref,
-    lin_other,
+    mod_w,
+    load_sem,
     lin_full,
     out_split,
-    mod_other,
+    mod_buf,
     mod_full,
+    gate_cols,
     fresh_in,
     xin,
     skip_out,
@@ -79,12 +82,22 @@
     half = sections // 2
     mirror = sections - 1 - s
     down = s < half
-    rows = inflow_ref.shape[1]
-    width = inflow_ref.shape[2]
+    rows = inflow_hbm.shape[1]
+    width = inflow_hbm.shape[2]
     half_width = width // 2
     heads = out_w_ref.shape[0] // DH
     head_cols = out_w_ref.shape[0]
     last = TICKS - 1
+
+    loads = [
+        pltpu.make_async_copy(inflow_hbm.at[c], xin.at[0], load_sem.at[0]),
+        pltpu.make_async_copy(mod_hbm, mod_w, load_sem.at[1]),
+        pltpu.make_async_copy(qkv_hbm, qkv_ref, load_sem.at[2]),
+        pltpu.make_async_copy(out_w_hbm, out_w_ref, load_sem.at[3]),
+        pltpu.make_async_copy(lin_ref, lin_full.at[c], load_sem.at[4]),
+    ]
+    for load in loads:
+        load.start()
 
     def remote(src, dst, send, recv, device):
         return pltpu.make_async_remote_copy(
@@ -148,25 +161,47 @@
 
     @pl.when(fresh_sender)
     def _():
-        for tick in range(TICKS - 1):
+        for tick in reversed(range(TICKS - 1)):
             fresh_copy(tick, s % half).start()
 
-    lin_copy = remote(lin_ref, lin_other, lin_sem.at[0], lin_sem.at[1], {"tensor": o})
-    mod_copy = remote(mod_ref, mod_other, mod_sem.at[0], mod_sem.at[1], {"tensor": o})
+    lin_copy = remote(lin_ref, lin_full.at[c], lin_sem.at[0], lin_sem.at[1], {"tensor": o})
+    mod_copy = remote(mod_buf.at[c], mod_buf.at[c], mod_sem.at[0], mod_sem.at[1], {"tensor": o})
+
+    lane = lax.broadcasted_iota(jnp.int32, (1, FREQ), 1)
+    entry = jnp.where(lane < FREQ // 2, lane, lane - FREQ // 2).astype(F32)
+    frequency = jnp.exp(-math.log(10000.0) * entry / (FREQ // 2))
+    tick_rows = lax.broadcasted_iota(jnp.int32, (8, FREQ), 0)
+    time_rows = jnp.zeros((8, FREQ), F32)
+    for tick in range(TICKS):
+        chosen = plan_ref[0, tick]
+        time = jnp.int32(0)
+        for micro in range(times_ref.shape[1]):
+            time = time + jnp.where(chosen == micro, times_ref[0, micro], 0)
+        time_rows = jnp.where(tick_rows == tick, time.astype(F32), time_rows)
+    phases = time_rows * frequency
+    embedded = jnp.where(lane < FREQ // 2, jnp.cos(phases), jnp.sin(phases))
+    loads[1].wait()
+    weights = mod_w[...]
+    high = embedded.astype(BF16)
+    rest = embedded - high.astype(F32)
+    middle = rest.astype(BF16)
+    low = (rest - middle.astype(F32)).astype(BF16)
+    mod_buf[c] = (
+        (dot_t(low, weights) + dot_t(middle, weights) + dot_t(high, weights))
+        .astype(BF16)
+        .astype(F32)
+    )
     mod_copy.start()
-
-    out_split[0] = out_w_ref[:, :half_width]
-    out_split[1] = out_w_ref[:, half_width:]
-    xin[0] = inflow_ref[c]
+    loads[0].wait()
+    gate_cols[...] = mod_buf[c][:, half_width:].T
     mod_copy.wait()
-
-    @pl.when(c == 0)
-    def _():
-        mod_full[...] = jnp.concatenate([mod_ref[...], mod_other[...]], axis=1)
-
-    @pl.when(c == 1)
-    def _():
-        mod_full[...] = jnp.concatenate([mod_other[...], mod_ref[...]], axis=1)
+    low_cols = mod_buf[0]
+    high_cols = mod_buf[1]
+    mod_full[0] = jnp.concatenate([low_cols[:, :half_width], high_cols[:, :half_width]], axis=1)
+    mod_full[1] = jnp.concatenate([low_cols[:, half_width:], high_cols[:, half_width:]], axis=1)
+
+    lin_copy.start()
+    loads[2].wait()
 
     def skip_copy(tick):
         return remote(
@@ -196,7 +231,7 @@
         ).wait_recv()
 
     def linear(tick):
-        return dot(xin[tick], lin_full[...])
+        return dot_t(xin[tick], lin_full[...].reshape(width, width))
 
     def fresh_arrive(tick):
         for block in range(half):
@@ -213,7 +248,11 @@
 
         @pl.when(c == 0)
         def _():
-            fresh_in[tick, 0] = fresh_ref[tick]
+            own_block = pltpu.make_async_copy(
+                fresh_ref.at[tick], fresh_in.at[tick, 0], fresh_recv.at[tick, 0]
+            )
+            own_block.start()
+            own_block.wait()
 
         xin[tick + 1] = fresh_in[tick].astype(F32).reshape(rows, width).astype(BF16)
 
@@ -234,7 +273,7 @@
             )
             top = jnp.max(scores, axis=-1, keepdims=True)
             grown = jnp.exp(scores - top)
-            soft = (grown / jnp.sum(grown, axis=-1, keepdims=True)).astype(BF16)
+            soft = (grown * (1.0 / jnp.sum(grown, axis=-1, keepdims=True))).astype(BF16)
             product = dot(soft, v)
             total = product if h == 0 else jnp.where(head_masks[h], product, total)
         return total.astype(BF16)
@@ -251,9 +290,10 @@
 
     def project(tick, part):
         rows_in = u_buf[tick, part]
-        q_buf[part] = dot(rows_in, qkv_ref[0]).astype(BF16)
-        k_buf[part] = dot(rows_in, qkv_ref[1]).astype(BF16)
-        v_buf[part] = dot(rows_in, qkv_ref[2]).astype(BF16)
+        projected = dot_t(rows_in, qkv_ref[...]).astype(BF16)
+        q_buf[part] = projected[:, :head_cols]
+        k_buf[part] = projected[:, head_cols : 2 * head_cols]
+        v_buf[part] = projected[:, 2 * head_cols :]
 
     def h_copy():
         return remote(h_cols.at[o], h_in, h_sem.at[0], h_sem.at[1], {"tensor": o})
@@ -263,13 +303,14 @@
         centred = values - jnp.mean(values, axis=-1, keepdims=True)
         variance = jnp.mean(centred * centred, axis=-1, keepdims=True)
         normed = centred * lax.rsqrt(variance + epsilon)
-        scaling = mod_full[2 * tick : 2 * tick + 1, :]
+        scaling = mod_full[0, tick : tick + 1, :]
         u_buf[tick, c] = (normed * (1.0 + scaling)).astype(BF16)
         u_copy(tick).start()
         project(tick, c)
         if tick == last:
-            h_cols[0] = hidden[:, :half_width]
-            h_cols[1] = hidden[:, half_width:]
+            turned = hidden[...].T
+            h_cols[0] = turned[:half_width]
+            h_cols[1] = turned[half_width:]
             h_copy().start()
         u_wait(tick)
         project(tick, o)
@@ -283,7 +324,7 @@
         g_out[tick] = dot(attend(o), out_w_ref[...]).astype(BF16)
         g_copy(tick).start()
         own = dot(attend(c), out_w_ref[...]).astype(BF16).astype(F32)
-        gating = mod_full[2 * tick + 1 : 2 * tick + 2, :]
+        gating = mod_full[1, tick : tick + 1, :]
         g_copy(tick).wait_recv()
         y = hidden[...] + gating * (own + g_in[tick].astype(F32))
         y_out[tick] = y.astype(BF16)
@@ -295,18 +336,21 @@
         )
 
     def settle():
-        gating = mod_ref[2 * last + 1 : 2 * last + 2, :]
+        gating = gate_cols[:, last : last + 1]
         for part in range(2):
             heads_out = attend(part)
-            gl_out[part] = dot(heads_out, out_split[o]).astype(BF16)
+            gl_out[part] = dot_t(out_split[o], heads_out).astype(BF16)
             gl_copy(part).start()
-            out_ref[part] = dot(heads_out, out_split[c]).astype(BF16).astype(F32)
+            out_ref[:, part * rows : (part + 1) * rows] = (
+                dot_t(out_split[c], heads_out).astype(BF16).astype(F32)
+            )
         h_copy().wait_recv()
         for part in range(2):
             gl_copy(part).wait_recv()
-            summed = out_ref[part] + gl_in[part].astype(F32)
+            where = slice(part * rows, (part + 1) * rows)
+            summed = out_ref[:, where] + gl_in[part].astype(F32)
             h_part = jnp.where(c == part, h_cols[c], h_in[...])
-            out_ref[part] = h_part + gating * summed
+            out_ref[:, where] = h_part + gating * summed
 
     def skip_needed(tick):
         return down & (mirror <= sections - TICKS + tick)
@@ -314,8 +358,6 @@
     def send_skip(tick):
         skip_out[tick] = linear(tick).astype(BF16)
         skip_copy(tick).start()
-
-    lin_copy.start()
 
     for tick in range(TICKS):
         live = s <= sections - TICKS + tick
@@ -325,23 +367,13 @@
             if tick > 0:
                 x_wait(tick - 1)
 
-        def prepare_linear():
-            lin_copy.wait()
-
-            @pl.when(c == 0)
-            def _():
-                lin_full[...] = jnp.concatenate([lin_ref[...], lin_other[...]], axis=1)
-
-            @pl.when(c == 1)
-            def _():
-                lin_full[...] = jnp.concatenate([lin_other[...], lin_ref[...]], axis=1)
-
         if tick == 0:
-            first_linear = skip_needed(0) | (jnp.logical_not(down))
+            first_linear = skip_needed(0) | jnp.logical_not(down)
 
             @pl.when(first_linear)
             def _():
-                prepare_linear()
+                loads[4].wait()
+                lin_copy.wait()
 
         if tick > 0:
 
@@ -371,6 +403,12 @@
             ).wait_recv()
             hidden[...] = own + skip_in[tick].astype(F32)
 
+        if tick == 0:
+            loads[3].wait()
+            turned_out = out_w_ref[...].astype(F32).T.astype(BF16)
+            out_split[0] = turned_out[:half_width]
+            out_split[1] = turned_out[half_width:]
+
         if tick < last:
 
             @pl.when(live)
@@ -386,13 +424,14 @@
 
             @pl.when(jnp.logical_not(first_linear))
             def _():
-                prepare_linear()
+                loads[4].wait()
+                lin_copy.wait()
 
             @pl.when(s == 0)
             def _():
-                for later in range(TICKS - 1):
+                for later in reversed(range(TICKS - 1)):
                     fresh_arrive(later)
-                for later in range(1, TICKS):
+                for later in reversed(range(1, TICKS)):
 
                     @pl.when(skip_needed(later))
                     def _():
@@ -428,33 +467,25 @@
     head_cols = out_weight.shape[1]
     half = sections // 2
     piece = fresh_rows.shape[2]
-    micro_ids = lax.broadcasted_iota(jnp.int32, (TICKS, timesteps.shape[0]), 1)
-    times = jnp.sum(jnp.where(micro_ids == plan, timesteps[:, 0][None, :], 0), axis=1)
-    modulation = (
-        jnp.einsum(
-            "tf,fcd->tcd",
-            timestep_embed(times),
-            mod_weight[0].astype(F32),
-            precision=lax.Precision.HIGHEST,
-        )
-        .astype(BF16)
-        .astype(F32)
-        .reshape(2 * TICKS, half_width)
-    )
-    modulation = jnp.pad(modulation, ((0, 8 - 2 * TICKS), (0, 0)))
     vmem = pl.BlockSpec(memory_space=pltpu.VMEM)
+    hbm = pl.BlockSpec(memory_space=pltpu.HBM)
+    smem = pl.BlockSpec(memory_space=pltpu.SMEM)
     dma = pltpu.SemaphoreType.DMA
     settled = pl.pallas_call(
         functools.partial(kernel, sections),
-        out_shape=jax.ShapeDtypeStruct((2, rows, half_width), F32),
-        in_specs=[vmem] * 6,
+        out_shape=jax.ShapeDtypeStruct((half_width, row_count), F32),
+        in_specs=[hbm] * 6 + [smem] * 2,
         out_specs=vmem,
         scratch_shapes=[
-            pltpu.VMEM((width, half_width), BF16),
-            pltpu.VMEM((width, width), BF16),
-            pltpu.VMEM((2, head_cols, half_width), BF16),
-            pltpu.VMEM((8, half_width), F32),
-            pltpu.VMEM((8, width), F32),
+            pltpu.VMEM((3 * head_cols, width), BF16),
+            pltpu.VMEM((head_cols, width), BF16),
+            pltpu.VMEM((2 * half_width, FREQ), BF16),
+            dma((5,)),
+            pltpu.VMEM((2, half_width, width), BF16),
+            pltpu.VMEM((2, half_width, head_cols), BF16),
+            pltpu.VMEM((2, 8, 2 * half_width), F32),
+            pltpu.VMEM((2, 8, width), F32),
+            pltpu.VMEM((half_width, 8), F32),
             pltpu.VMEM((TICKS - 1, half, piece, width), BF16),
             pltpu.VMEM((TICKS, rows, width), BF16),
             pltpu.VMEM((TICKS, rows, width), BF16),
@@ -466,10 +497,10 @@
             pltpu.VMEM((2, rows, head_cols), BF16),
             pltpu.VMEM((TICKS - 1, rows, width), BF16),
             pltpu.VMEM((TICKS - 1, rows, width), BF16),
-            pltpu.VMEM((2, rows, half_width), BF16),
-            pltpu.VMEM((2, rows, half_width), BF16),
-            pltpu.VMEM((2, rows, half_width), F32),
-            pltpu.VMEM((rows, half_width), F32),
+            pltpu.VMEM((2, half_width, rows), BF16),
+            pltpu.VMEM((2, half_width, rows), BF16),
+            pltpu.VMEM((2, half_width, rows), F32),
+            pltpu.VMEM((half_width, rows), F32),
             pltpu.VMEM((TICKS - 1, rows, width), BF16),
             dma((2,)),
             dma((2,)),
@@ -488,17 +519,19 @@
             dma((2,)),
         ],
         compiler_params=pltpu.CompilerParams(
-            collective_id=0, has_side_effects=True, vmem_limit_bytes=44 * 2**20
+            collective_id=0, has_side_effects=True, vmem_limit_bytes=63 * 2**20
         ),
     )(
         inflow[0].reshape(2, rows, width),
         fresh_rows[:, 0],
-        lin_weight[0],
-        qkv_weight[0],
+        lin_weight[0].T,
+        qkv_weight[0].transpose(0, 2, 1).reshape(3 * head_cols, width),
         out_weight[0],
-        modulation,
+        mod_weight[0].transpose(1, 2, 0).reshape(2 * half_width, FREQ),
+        plan.T,
+        timesteps.T,
     )
-    return settled.reshape(1, row_count, half_width)
+    return settled.T[None]
 
 
 def solution(mesh):

time: 72.6 us -> 62.6 us (0.86)
  local copies, waits for them, and re-layouts: 12.8 us -> 1.92 us
  Pallas kernels: 57.2 us -> 60.5 us
  other arithmetic: 1.64 us -> 0 us
    unnamed x16 -> x1, local copies, waits for them, and re-layouts: 10.7 us -> 1.92 us
    pallas_call x1, Pallas kernels: 57.2 us -> 60.5 us  [on_device(): pl.pallas_call(functools.partial(kernel, sections), out_shape=jax.ShapeDt...]
    reshape x2 -> x0, local copies, waits for them, and re-layouts: 2.14 us -> none  [the longest x1 2.12 us: on_device(): return settled.reshape(1, row_count, half_width)]
    reduce_sum x1 -> x0, other arithmetic: 0.9 us -> none  [on_device(): jnp.sum(jnp.where(micro_ids == plan, timesteps[:, 0][None, :], 0), axis=1)]
where the time goes in v2:
time: 62.6 us; the launch traced here: 62.4 us
  Pallas kernels  60.5 us (97%)
  local copies, waits for them, and re-layouts  1.92 us (3%)
    pallas_call x1, Pallas kernels, on_device(): pl.pallas_call(functools.partial(kernel, sections), out_shape=jax.ShapeDt...  60.5 us
    unnamed x1, local copies, waits for them, and re-layouts  1.92 us

profile of v2, /device:TPU:29, one launch (start us, length us, event | category | flops | bytes accessed | tf_op | source)
XLA Modules:
  0.0 62.4 jit_solution(1980303010911515021)
XLA Ops:
  0.0 60.5 %shard_map.82 = f32[576,256]{1,0:T(8,128)} custom-call(bf16[2,128,1152]{2,1,0:T(8,128)(2,1)} %bitcast.25, bf16[2,64,1152]{2,1,0:T(8,128)(2,1)} %bitcast.26, bf16[576,1152]{1,0:T(8,128)(2,1)} %bitcast.23, bf16[864,1152]{1,0:T(8,128)(2,1)} %bitcast.22, bf16[288,1152]{1,0:T(8,128)(2,1)} %bitcast.24, bf16[1152,128]{1,0:T(8,128)(2,1)} %bitcast.27, ...), custom_call_target="tpu_custom_call" | custom-call | tf_op jit(solution)/shard_map/pallas_call | solution.py:474
  60.5 1.9 %copy.10 = f32[1,256,576]{1,2,0:T(8,128)} copy(f32[1,256,576]{1,2,0:T(8,128)} %bitcast.21) | data formatting | bytes 1179648

commit v3 on v2

--- a/solution.py
+++ b/solution.py
@@ -161,7 +161,7 @@
 
     @pl.when(fresh_sender)
     def _():
-        for tick in reversed(range(TICKS - 1)):
+        for tick in range(TICKS - 1):
             fresh_copy(tick, s % half).start()
 
     lin_copy = remote(lin_ref, lin_full.at[c], lin_sem.at[0], lin_sem.at[1], {"tensor": o})
@@ -375,17 +375,14 @@
                 loads[4].wait()
                 lin_copy.wait()
 
-        if tick > 0:
-
-            @pl.when(skip_needed(tick) & (s > 0))
-            def _():
-                send_skip(tick)
-
-        else:
-
-            @pl.when(skip_needed(tick))
-            def _():
-                send_skip(tick)
+        if tick == last:
+            @pl.when(s == 0)
+            def _():
+                x_copy(last - 1).wait_send()
+
+        @pl.when(skip_needed(tick))
+        def _():
+            send_skip(tick)
 
         @pl.when(live & down)
         def _():
@@ -429,13 +426,8 @@
 
             @pl.when(s == 0)
             def _():
-                for later in reversed(range(TICKS - 1)):
+                for later in range(TICKS - 1):
                     fresh_arrive(later)
-                for later in reversed(range(1, TICKS)):
-
-                    @pl.when(skip_needed(later))
-                    def _():
-                        send_skip(later)
 
     @pl.when(fresh_sender)
     def _():
@@ -456,7 +448,13 @@
             u_copy(tick).wait_send()
             if tick < last:
                 g_copy(tick).wait_send()
-                x_copy(tick).wait_send()
+                if tick < last - 1:
+                    x_copy(tick).wait_send()
+                else:
+
+                    @pl.when(s > 0)
+                    def _():
+                        x_copy(tick).wait_send()
 
 
 def on_device(inflow, fresh_rows, lin_weight, qkv_weight, out_weight, mod_weight, plan, timesteps):
@@ -519,7 +517,7 @@
             dma((2,)),
         ],
         compiler_params=pltpu.CompilerParams(
-            collective_id=0, has_side_effects=True, vmem_limit_bytes=63 * 2**20
+            collective_id=0, has_side_effects=True, vmem_limit_bytes=62 * 2**20 + 2**18
         ),
     )(
         inflow[0].reshape(2, rows, width),

time: 62.6 us -> 62.5 us (level)
  the two profiles are of different devices: /device:TPU:29 before, /device:TPU:23 now
where the time goes in v3:
time: 62.5 us; the launch traced here: 62.3 us
  Pallas kernels  60.4 us (97%)
  local copies, waits for them, and re-layouts  1.92 us (3%)
    pallas_call x1, Pallas kernels, on_device(): pl.pallas_call(functools.partial(kernel, sections), out_shape=jax.ShapeDt...  60.4 us
    unnamed x1, local copies, waits for them, and re-layouts  1.92 us

profile of v3, /device:TPU:23, one launch (start us, length us, event | category | flops | bytes accessed | tf_op | source)
XLA Modules:
  0.0 62.3 jit_solution(10838077258127833265)
XLA Ops:
  0.0 60.4 %shard_map.82 = f32[576,256]{1,0:T(8,128)} custom-call(bf16[2,128,1152]{2,1,0:T(8,128)(2,1)} %bitcast.25, bf16[2,64,1152]{2,1,0:T(8,128)(2,1)} %bitcast.26, bf16[576,1152]{1,0:T(8,128)(2,1)} %bitcast.23, bf16[864,1152]{1,0:T(8,128)(2,1)} %bitcast.22, bf16[288,1152]{1,0:T(8,128)(2,1)} %bitcast.24, bf16[1152,128]{1,0:T(8,128)(2,1)} %bitcast.27, ...), custom_call_target="tpu_custom_call" | custom-call | tf_op jit(solution)/shard_map/pallas_call | solution.py:472
  60.4 1.9 %copy.10 = f32[1,256,576]{1,2,0:T(8,128)} copy(f32[1,256,576]{1,2,0:T(8,128)} %bitcast.21) | data formatting | bytes 1179648

commit v4 on v3

--- a/solution.py
+++ b/solution.py
@@ -193,14 +193,12 @@
     )
     mod_copy.start()
     loads[0].wait()
-    gate_cols[...] = mod_buf[c][:, half_width:].T
     mod_copy.wait()
     low_cols = mod_buf[0]
     high_cols = mod_buf[1]
     mod_full[0] = jnp.concatenate([low_cols[:, :half_width], high_cols[:, :half_width]], axis=1)
     mod_full[1] = jnp.concatenate([low_cols[:, half_width:], high_cols[:, half_width:]], axis=1)
 
-    lin_copy.start()
     loads[2].wait()
 
     def skip_copy(tick):
@@ -368,19 +366,22 @@
                 x_wait(tick - 1)
 
         if tick == 0:
-            first_linear = skip_needed(0) | jnp.logical_not(down)
+            first_linear = skip_needed(0) | (jnp.logical_not(down) & live)
 
             @pl.when(first_linear)
             def _():
+                lin_copy.start()
                 loads[4].wait()
                 lin_copy.wait()
 
-        if tick == last:
-            @pl.when(s == 0)
-            def _():
-                x_copy(last - 1).wait_send()
-
-        @pl.when(skip_needed(tick))
+        if tick == 1:
+
+            @pl.when(jnp.logical_not(first_linear) & (s > 0))
+            def _():
+                loads[4].wait()
+                lin_copy.wait()
+
+        @pl.when(skip_needed(tick) & (s > 0))
         def _():
             send_skip(tick)
 
@@ -402,27 +403,36 @@
 
         if tick == 0:
             loads[3].wait()
+
+        if tick < last:
+
+            @pl.when(live)
+            def _():
+                block(tick)
+                if tick == last - 1:
+                    @pl.when(s == 0)
+                    def _():
+                        loads[4].wait()
+                        lin_copy.wait()
+                        x_copy(0).wait_send()
+                        send_skip(last)
+
+                relay(tick)
+
+        else:
+            block(tick)
+            settle()
+
+        if tick == 0:
+
+            @pl.when(jnp.logical_not(first_linear))
+            def _():
+                lin_copy.start()
+
             turned_out = out_w_ref[...].astype(F32).T.astype(BF16)
             out_split[0] = turned_out[:half_width]
             out_split[1] = turned_out[half_width:]
-
-        if tick < last:
-
-            @pl.when(live)
-            def _():
-                block(tick)
-                relay(tick)
-
-        else:
-            block(tick)
-            settle()
-
-        if tick == 0:
-
-            @pl.when(jnp.logical_not(first_linear))
-            def _():
-                loads[4].wait()
-                lin_copy.wait()
+            gate_cols[...] = mod_buf[c][:, half_width:].T
 
             @pl.when(s == 0)
             def _():
@@ -448,7 +458,7 @@
             u_copy(tick).wait_send()
             if tick < last:
                 g_copy(tick).wait_send()
-                if tick < last - 1:
+                if tick > 0:
                     x_copy(tick).wait_send()
                 else:
 

time: 62.5 us -> 62 us (level)
  the two profiles are of different devices: /device:TPU:23 before, /device:TPU:29 now
where the time goes in v4:
time: 62 us; the launch traced here: 61.8 us
  Pallas kernels  59.9 us (97%)
  local copies, waits for them, and re-layouts  1.92 us (3%)
    pallas_call x1, Pallas kernels, on_device(): pl.pallas_call(functools.partial(kernel, sections), out_shape=jax.ShapeDt...  59.9 us
    unnamed x1, local copies, waits for them, and re-layouts  1.92 us

profile of v4, /device:TPU:29, one launch (start us, length us, event | category | flops | bytes accessed | tf_op | source)
XLA Modules:
  0.0 61.8 jit_solution(2624955984667225053)
XLA Ops:
  0.0 59.9 %shard_map.82 = f32[576,256]{1,0:T(8,128)} custom-call(bf16[2,128,1152]{2,1,0:T(8,128)(2,1)} %bitcast.25, bf16[2,64,1152]{2,1,0:T(8,128)(2,1)} %bitcast.26, bf16[576,1152]{1,0:T(8,128)(2,1)} %bitcast.23, bf16[864,1152]{1,0:T(8,128)(2,1)} %bitcast.22, bf16[288,1152]{1,0:T(8,128)(2,1)} %bitcast.24, bf16[1152,128]{1,0:T(8,128)(2,1)} %bitcast.27, ...), custom_call_target="tpu_custom_call" | custom-call | tf_op jit(solution)/shard_map/pallas_call | solution.py:482
  59.9 1.9 %copy.10 = f32[1,256,576]{1,2,0:T(8,128)} copy(f32[1,256,576]{1,2,0:T(8,128)} %bitcast.21) | data formatting | bytes 1179648
